TPU v7x, 32 devices: a whole 2x2x4 slice. The times are simulated.
32 devices in a mesh: tm: 16 (over z, x, core), space: 2 (over y).
Axes of the slice: x: 2, y: 2, z: 4, core: 2. Of those that a mesh axis runs over, the one named last changes fastest.
Arguments:
- primal: float32 [128, 5, 16, 16, 128], P('tm', None, 'space'), may hold values from -2 to 2
- source: float32 [128, 5, 16, 16, 128], P('tm', None, 'space'), may hold values from -4 to 4
- guess: float32 [16, 5, 16, 16, 128], P('tm', None, 'space'), may hold values from -6 to 6
- mixing: float32 [5, 5], replicated, may hold values from -1 to 1.2
Outputs:
- fine_states: float32 [128, 5, 16, 16, 128], P('tm', None, 'space')
- coarse_residual: float32 [16, 5, 16, 16, 128], P('tm', None, 'space')
All inputs are finite; a program needn't handle non-finite values.
Results may differ from a plain program's by a relative error of at most 0.00026.
Values sent between devices are 32-bit elements; how exact they have to be, the bound alone decides.
A program may use at most 64 MiB of HBM per device.

v0:
```python
import functools

import jax
import jax.numpy as jnp
from jax import lax
from jax.experimental import pallas as pl
from jax.experimental.pallas import tpu as pltpu
from jax.sharding import PartitionSpec as P

DIFFUSION = 0.1
RATE = 0.25
COARSE_STEP = 0.75
KEEP = 1.0 - 6.0 * DIFFUSION - RATE
MESH = pl.DeviceIdType.MESH
LEFT, RIGHT = 0, 1


def kernel(blocks, slabs, primal_hbm, source_hbm, guess, mixing, fine, residual_out,
           primal, source, scaled, state, halo, ends, end_in, relaxed, moved, moved_in,
           load_p, load_s, halo_send, halo_recv, end_send, end_recv, err_send, err_recv):
    steps, fields, nx, ny, nz = primal.shape
    last = nx - 1
    position = lax.axis_index("tm")
    slab = lax.axis_index("space")
    side = {LEFT: lax.rem(slab + slabs - 1, slabs), RIGHT: lax.rem(slab + 1, slabs)}
    edge = {LEFT: 0, RIGHT: last}
    first_block = position == 0
    has_next = position < blocks - 1
    groups = halo_send.shape[-1]
    cuts = [(g * fields) // groups for g in range(groups + 1)]

    def load_primal(t):
        return pltpu.make_async_copy(primal_hbm.at[t], primal.at[t], load_p.at[t])

    def load_source(t):
        return pltpu.make_async_copy(source_hbm.at[t], source.at[t], load_s.at[t])

    load_primal(0).start()
    load_source(0).start()
    for t in range(1, steps):
        load_source(t).start()
        load_primal(t).start()

    barrier = pltpu.get_barrier_semaphore()
    for way in (LEFT, RIGHT):
        pl.semaphore_signal(barrier, inc=1, device_id={"space": side[way]}, device_id_type=MESH)

    @pl.when(has_next)
    def _():
        pl.semaphore_signal(barrier, inc=1, device_id={"tm": position + 1}, device_id_type=MESH)

    @pl.when(jnp.logical_not(first_block))
    def _():
        pl.semaphore_signal(barrier, inc=1, device_id={"tm": position - 1}, device_id_type=MESH)

    pl.semaphore_wait(barrier, 2 + jnp.where(first_block, 0, 1) + jnp.where(has_next, 1, 0))

    weights = [[mixing[i, j] for j in range(fields)] for i in range(fields)]

    def mix(values, i):
        total = weights[i][0] * values[0]
        for j in range(1, fields):
            total = total + weights[i][j] * values[j]
        return total

    rows = lax.broadcasted_iota(jnp.int32, (ny, nz), 0)
    top, bottom = rows == 0, rows == ny - 1

    def halo_copy(way, slot, g):
        part = pl.ds(cuts[g], cuts[g + 1] - cuts[g])
        return pltpu.make_async_remote_copy(
            src_ref=state.at[slot, edge[way], part],
            dst_ref=halo.at[way, slot, part],
            send_sem=halo_send.at[way, slot, g],
            recv_sem=halo_recv.at[way, slot, g],
            device_id={"space": side[way]},
            device_id_type=MESH,
        )

    def end_copy(m, x):
        return pltpu.make_async_remote_copy(
            src_ref=ends.at[m, x], dst_ref=end_in.at[m, x],
            send_sem=end_send.at[m, x], recv_sem=end_recv.at[m, x],
            device_id={"tm": position + 1}, device_id_type=MESH,
        )

    def err_copy(x):
        return pltpu.make_async_remote_copy(
            src_ref=moved.at[x], dst_ref=moved_in.at[x],
            send_sem=err_send.at[x], recv_sem=err_recv.at[x],
            device_id={"tm": position + 1}, device_id_type=MESH,
        )

    def stepped(slot, t, x, near):
        values = [state[slot, x, f] for f in range(fields)]
        results = []
        for f in range(fields):
            v = values[f]
            around = jnp.where(top, 0.0, pltpu.roll(v, 1, 0))
            around = around + jnp.where(bottom, 0.0, pltpu.roll(v, ny - 1, 0))
            around = around + pltpu.roll(v, 1, 1) + pltpu.roll(v, nz - 1, 1)
            for other in near:
                around = around + state[slot, other, f]
            results.append(KEEP * v + DIFFUSION * around + scaled[t, f, x] * mix(values, f))
        return results

    def step(m, slot, t, ways, closing):
        final = m == 2

        def put(x, f, value):
            if closing and not final:
                ends[m, x, f] = value
                return
            value = value + source[t + 1, f, x]
            if final:
                fine[t + 1, f, x] = value
            if not closing:
                state[1 - slot, x, f] = value

        if m == 0:
            load_primal(t).wait()
            if not closing:
                load_source(t + 1).wait()

            def slope(x, carry):
                values = [primal[t, f, x] for f in range(fields)]
                for f in range(fields):
                    bent = jnp.tanh(mix(values, f))
                    scaled[t, f, x] = RATE - RATE * (bent * bent)
                return carry

            lax.fori_loop(0, nx, slope, 0)

        def inner(x, carry):
            results = stepped(slot, t, x, (x - 1, x + 1))
            for f in range(fields):
                put(x, f, results[f])
            if closing and not final:
                @pl.when(has_next)
                def _():
                    end_copy(m, x).start()
            return carry

        lax.fori_loop(1, last, inner, 0)
        for way in ways:
            target = RIGHT if way == LEFT else LEFT
            x = edge[target]
            results = stepped(slot, t, x, (x + 1 if target == LEFT else x - 1,))
            for g in range(groups):
                halo_copy(way, slot, g).wait_recv()
                for f in range(cuts[g], cuts[g + 1]):
                    put(x, f, results[f] + DIFFUSION * halo[way, slot, f])
                if not closing:
                    halo_copy(target, 1 - slot, g).start()
            if closing and not final:
                @pl.when(has_next)
                def _():
                    end_copy(m, x).start()
        for way in ways:
            for g in range(groups):
                halo_copy(way, slot, g).wait_send()

    forward, backward = (LEFT, RIGHT), (RIGHT, LEFT)

    def march(m, count):
        pairs = (count - 1) // 2

        def pair(i, carry):
            step(m, 0, 2 * i, forward, False)
            step(m, 1, 2 * i + 1, backward, False)
            return carry

        lax.fori_loop(0, pairs, pair, 0)
        for t in range(2 * pairs, count):
            step(m, t % 2, t, (forward, backward)[t % 2], t == count - 1)

    def send_edge(way):
        for g in range(groups):
            halo_copy(way, 0, g).start()

    def begin(place):
        place(edge[LEFT])
        send_edge(LEFT)
        place(edge[RIGHT])
        send_edge(RIGHT)

        def rest(x, carry):
            place(x)
            return carry

        lax.fori_loop(1, last, rest, 0)

    def from_guess(x):
        for f in range(fields):
            state[0, x, f] = guess[0, f, x]

    begin(from_guess)
    load_source(0).wait()
    march(0, steps)

    def from_end(x):
        @pl.when(first_block)
        def _():
            for f in range(fields):
                value = guess[0, f, x]
                state[0, x, f] = value
                relaxed[x, f] = value

        @pl.when(jnp.logical_not(first_block))
        def _():
            end_copy(0, x).wait_recv()
            for f in range(fields):
                value = end_in[0, x, f] + source[0, f, x]
                state[0, x, f] = value
                relaxed[x, f] = value

    begin(from_end)
    march(1, steps)

    def from_error(x):
        @pl.when(first_block)
        def _():
            for f in range(fields):
                value = source[0, f, x]
                residual_out[0, f, x] = value
                moved_in[x, f] = value

        @pl.when(jnp.logical_not(first_block))
        def _():
            end_copy(1, x).wait_recv()
            rest = []
            for f in range(fields):
                value = end_in[1, x, f] + source[0, f, x] - relaxed[x, f]
                residual_out[0, f, x] = value
                rest.append(value)
            err_copy(x).wait_recv()
            for f in range(fields):
                moved_in[x, f] = moved_in[x, f] + rest[f]

        error = [moved_in[x, f] for f in range(fields)]

        @pl.when(has_next)
        def _():
            for f in range(fields):
                moved[x, f] = (1.0 - COARSE_STEP) * error[f] + (COARSE_STEP / RATE) * (
                    scaled[0, f, x] * mix(error, f))
            err_copy(x).start()

        for f in range(fields):
            value = relaxed[x, f] + error[f]
            state[0, x, f] = value
            fine[0, f, x] = value

    begin(from_error)
    march(2, steps - 1)

    @pl.when(has_next)
    def _():
        def drain(x, carry):
            end_copy(0, x).wait_send()
            end_copy(1, x).wait_send()
            err_copy(x).wait_send()
            return carry

        lax.fori_loop(0, nx, drain, 0)


def per_device(blocks, slabs, primal, source, guess, mixing):
    steps, fields, nx, ny, nz = primal.shape
    groups = 2
    plane = (nx, fields, ny, nz)
    vmem = pl.BlockSpec(memory_space=pltpu.VMEM)
    dma = pltpu.SemaphoreType.DMA
    f32 = jnp.float32
    return pl.pallas_call(
        functools.partial(kernel, blocks, slabs),
        out_shape=(jax.ShapeDtypeStruct(primal.shape, f32), jax.ShapeDtypeStruct(guess.shape, f32)),
        in_specs=[pl.BlockSpec(memory_space=pl.ANY)] * 2
        + [vmem, pl.BlockSpec(memory_space=pltpu.SMEM)],
        out_specs=(vmem, vmem),
        scratch_shapes=[
            pltpu.VMEM(primal.shape, f32),
            pltpu.VMEM(primal.shape, f32),
            pltpu.VMEM(primal.shape, f32),
            pltpu.VMEM((2,) + plane, f32),
            pltpu.VMEM((2, 2, fields, ny, nz), f32),
            pltpu.VMEM((2,) + plane, f32),
            pltpu.VMEM((2,) + plane, f32),
            pltpu.VMEM(plane, f32),
            pltpu.VMEM(plane, f32),
            pltpu.VMEM(plane, f32),
            dma((steps,)),
            dma((steps,)),
            dma((2, 2, groups)),
            dma((2, 2, groups)),
            dma((2, nx)),
            dma((2, nx)),
            dma((nx,)),
            dma((nx,)),
        ],
        compiler_params=pltpu.CompilerParams(
            collective_id=0, has_side_effects=True, vmem_limit_bytes=40 * 2**20),
    )(primal, source, guess, mixing)


def solution(mesh):
    placed = P("tm", None, "space", None, None)
    return jax.shard_map(
        functools.partial(per_device, mesh.shape["tm"], mesh.shape["space"]),
        mesh=mesh,
        in_specs=(placed, placed, placed, P()),
        out_specs=(placed, placed),
        check_vma=False,
    )
```

profile of v0, /device:TPU:26, one launch (start us, length us, event | category | flops | bytes accessed | tf_op | source)
XLA Modules:
  0.0 108.4 jit_solution(1250208652765606426)
XLA Ops:
  0.6 0.0 copy-start
  0.6 1.7 %copy-done = f32[8,5,8,16,128]{4,3,2,1,0:T(8,128)S(1)} copy-done((f32[8,5,8,16,128]{4,3,2,1,0:T(8,128)S(1)}, f32[8,5,8,16,128]{4,3,2,1,0:T(8,128)}, u32[]{:S(2)}) %copy-start) | copy-done | bytes 2621464
  2.4 0.0 copy-start.1
  2.4 1.7 %copy-done.1 = f32[8,5,8,16,128]{4,3,2,1,0:T(8,128)S(1)} copy-done((f32[8,5,8,16,128]{4,3,2,1,0:T(8,128)S(1)}, f32[8,5,8,16,128]{4,3,2,1,0:T(8,128)}, u32[]{:S(2)}) %copy-start.1) | copy-done | bytes 2621464
  4.1 0.0 copy-start.2
  4.1 1.0 copy-done.2
  5.1 0.0 copy-start.3
  5.1 0.7 copy-done.3
  5.8 100.4 %shard_map.59 = (f32[8,5,8,16,128]{4,3,2,1,0:T(8,128)S(1)}, f32[1,5,8,16,128]{4,3,2,1,0:T(8,128)S(1)}) custom-call(f32[8,5,8,16,128]{4,3,2,1,0:T(8,128)S(1)} %copy-done, f32[8,5,8,16,128]{4,3,2,1,0:T(8,128)S(1)} %copy-done.1, f32[1,5,8,16,128]{4,3,2,1,0:T(8,128)S(1)} %copy-done.2, f32[5,5]{1,0:T(8,128)S(1)} %copy-done.3), custom_call_target="tpu_custom_call" | custom-call | tf_op jit(solution)/shard_map/pallas_call | solution.py:275
  106.1 1.5 %copy.8 = f32[8,5,8,16,128]{4,3,2,1,0:T(8,128)} copy(f32[8,5,8,16,128]{4,3,2,1,0:T(8,128)S(1)} %get-tuple-element.4) | data formatting | bytes 5242880
  107.6 0.7 copy.9
Async XLA Ops:
  0.6 1.7 %copy-start = (f32[8,5,8,16,128]{4,3,2,1,0:T(8,128)S(1)}, f32[8,5,8,16,128]{4,3,2,1,0:T(8,128)}, u32[]{:S(2)}) copy-start(f32[8,5,8,16,128]{4,3,2,1,0:T(8,128)} %primal_hbm.1) | copy-start | bytes 7864324
  2.4 1.7 %copy-start.1 = (f32[8,5,8,16,128]{4,3,2,1,0:T(8,128)S(1)}, f32[8,5,8,16,128]{4,3,2,1,0:T(8,128)}, u32[]{:S(2)}) copy-start(f32[8,5,8,16,128]{4,3,2,1,0:T(8,128)} %source_hbm.1) | copy-start | bytes 7864324
  4.1 1.0 copy-start.2
  5.1 0.7 copy-start.3
where the time goes:
time: 109 us; the launch traced here: 108 us
  Pallas kernels  100 us (92%)
  local copies, waits for them, and re-layouts  7.35 us (7%)
    pallas_call x1, Pallas kernels, per_device(): pl.pallas_call(functools.partial(kernel, blocks, slabs), out_shape=(jax.S...  100 us
    unnamed x10, local copies, waits for them, and re-layouts  7.35 us

commit v1 on v0

--- a/solution.py
+++ b/solution.py
@@ -13,11 +13,12 @@
 KEEP = 1.0 - 6.0 * DIFFUSION - RATE
 MESH = pl.DeviceIdType.MESH
 LEFT, RIGHT = 0, 1
-
-
-def kernel(blocks, slabs, primal_hbm, source_hbm, guess, mixing, fine, residual_out,
-           primal, source, scaled, state, halo, ends, end_in, relaxed, moved, moved_in,
-           load_p, load_s, halo_send, halo_recv, end_send, end_recv, err_send, err_recv):
+PAD = 8
+
+
+def kernel(blocks, slabs, primal_hbm, source_hbm, guess_hbm, mixing, fine_hbm, residual_hbm,
+           primal, source, guess, fine, residual_out, scaled, state, halo, ends, end_in, relaxed, moved, moved_in,
+           load_p, load_s, load_g, store_f, store_r, halo_send, halo_recv, end_send, end_recv, err_send, err_recv):
     steps, fields, nx, ny, nz = primal.shape
     last = nx - 1
     position = lax.axis_index("tm")
@@ -35,6 +36,12 @@
     def load_source(t):
         return pltpu.make_async_copy(source_hbm.at[t], source.at[t], load_s.at[t])
 
+    def store_fine(t):
+        return pltpu.make_async_copy(fine.at[t], fine_hbm.at[t], store_f.at[t])
+
+    load_guess = pltpu.make_async_copy(guess_hbm, guess, load_g)
+    store_residual = pltpu.make_async_copy(residual_out, residual_hbm, store_r)
+    load_guess.start()
     load_primal(0).start()
     load_source(0).start()
     for t in range(1, steps):
@@ -63,13 +70,22 @@
             total = total + weights[i][j] * values[j]
         return total
 
-    rows = lax.broadcasted_iota(jnp.int32, (ny, nz), 0)
-    top, bottom = rows == 0, rows == ny - 1
+    body = pl.ds(PAD, ny)
+    blank = jnp.zeros((PAD, nz), jnp.float32)
+
+    def clear(x, carry):
+        for slot in range(2):
+            for f in range(fields):
+                state[slot, x, f, pl.ds(0, PAD)] = blank
+                state[slot, x, f, pl.ds(PAD + ny, PAD)] = blank
+        return carry
+
+    lax.fori_loop(0, nx, clear, 0)
 
     def halo_copy(way, slot, g):
         part = pl.ds(cuts[g], cuts[g + 1] - cuts[g])
         return pltpu.make_async_remote_copy(
-            src_ref=state.at[slot, edge[way], part],
+            src_ref=state.at[slot, edge[way], part, body],
             dst_ref=halo.at[way, slot, part],
             send_sem=halo_send.at[way, slot, g],
             recv_sem=halo_recv.at[way, slot, g],
@@ -92,30 +108,32 @@
         )
 
     def stepped(slot, t, x, near):
-        values = [state[slot, x, f] for f in range(fields)]
+        values = [state[slot, x, f, body] for f in range(fields)]
         results = []
         for f in range(fields):
             v = values[f]
-            around = jnp.where(top, 0.0, pltpu.roll(v, 1, 0))
-            around = around + jnp.where(bottom, 0.0, pltpu.roll(v, ny - 1, 0))
-            around = around + pltpu.roll(v, 1, 1) + pltpu.roll(v, nz - 1, 1)
+            around = pltpu.roll(v, 1, 1) + pltpu.roll(v, nz - 1, 1)
+            around = around + state[slot, x, f, pl.ds(PAD - 1, ny)]
+            around = around + state[slot, x, f, pl.ds(PAD + 1, ny)]
             for other in near:
-                around = around + state[slot, other, f]
+                around = around + state[slot, other, f, body]
             results.append(KEEP * v + DIFFUSION * around + scaled[t, f, x] * mix(values, f))
         return results
 
     def step(m, slot, t, ways, closing):
         final = m == 2
+
+        def given(x, f, value):
+            return value if closing and not final else value + source[t + 1, f, x]
 
         def put(x, f, value):
             if closing and not final:
                 ends[m, x, f] = value
                 return
-            value = value + source[t + 1, f, x]
             if final:
                 fine[t + 1, f, x] = value
             if not closing:
-                state[1 - slot, x, f] = value
+                state[1 - slot, x, f, body] = value
 
         if m == 0:
             load_primal(t).wait()
@@ -129,23 +147,27 @@
                     scaled[t, f, x] = RATE - RATE * (bent * bent)
                 return carry
 
-            lax.fori_loop(0, nx, slope, 0)
+            lax.fori_loop(0, nx, slope, 0, unroll=2)
 
         def inner(x, carry):
             results = stepped(slot, t, x, (x - 1, x + 1))
             for f in range(fields):
-                put(x, f, results[f])
+                put(x, f, given(x, f, results[f]))
             if closing and not final:
                 @pl.when(has_next)
                 def _():
                     end_copy(m, x).start()
             return carry
 
-        lax.fori_loop(1, last, inner, 0)
+        for x in range(1, last):
+            inner(x, 0)
+        waiting = []
         for way in ways:
             target = RIGHT if way == LEFT else LEFT
             x = edge[target]
             results = stepped(slot, t, x, (x + 1 if target == LEFT else x - 1,))
+            waiting.append((way, target, x, [given(x, f, results[f]) for f in range(fields)]))
+        for way, target, x, results in waiting:
             for g in range(groups):
                 halo_copy(way, slot, g).wait_recv()
                 for f in range(cuts[g], cuts[g + 1]):
@@ -159,6 +181,8 @@
         for way in ways:
             for g in range(groups):
                 halo_copy(way, slot, g).wait_send()
+        if final:
+            store_fine(t + 1).start()
 
     forward, backward = (LEFT, RIGHT), (RIGHT, LEFT)
 
@@ -192,8 +216,9 @@
 
     def from_guess(x):
         for f in range(fields):
-            state[0, x, f] = guess[0, f, x]
-
+            state[0, x, f, body] = guess[0, f, x]
+
+    load_guess.wait()
     begin(from_guess)
     load_source(0).wait()
     march(0, steps)
@@ -203,7 +228,7 @@
         def _():
             for f in range(fields):
                 value = guess[0, f, x]
-                state[0, x, f] = value
+                state[0, x, f, body] = value
                 relaxed[x, f] = value
 
         @pl.when(jnp.logical_not(first_block))
@@ -211,7 +236,7 @@
             end_copy(0, x).wait_recv()
             for f in range(fields):
                 value = end_in[0, x, f] + source[0, f, x]
-                state[0, x, f] = value
+                state[0, x, f, body] = value
                 relaxed[x, f] = value
 
     begin(from_end)
@@ -248,11 +273,16 @@
 
         for f in range(fields):
             value = relaxed[x, f] + error[f]
-            state[0, x, f] = value
+            state[0, x, f, body] = value
             fine[0, f, x] = value
 
     begin(from_error)
+    store_fine(0).start()
+    store_residual.start()
     march(2, steps - 1)
+    for t in range(steps):
+        store_fine(t).wait()
+    store_residual.wait()
 
     @pl.when(has_next)
     def _():
@@ -269,20 +299,23 @@
     steps, fields, nx, ny, nz = primal.shape
     groups = 2
     plane = (nx, fields, ny, nz)
-    vmem = pl.BlockSpec(memory_space=pltpu.VMEM)
+    padded = (nx, fields, ny + 2 * PAD, nz)
+    anywhere = pl.BlockSpec(memory_space=pl.ANY)
     dma = pltpu.SemaphoreType.DMA
     f32 = jnp.float32
     return pl.pallas_call(
         functools.partial(kernel, blocks, slabs),
         out_shape=(jax.ShapeDtypeStruct(primal.shape, f32), jax.ShapeDtypeStruct(guess.shape, f32)),
-        in_specs=[pl.BlockSpec(memory_space=pl.ANY)] * 2
-        + [vmem, pl.BlockSpec(memory_space=pltpu.SMEM)],
-        out_specs=(vmem, vmem),
+        in_specs=[anywhere] * 3 + [pl.BlockSpec(memory_space=pltpu.SMEM)],
+        out_specs=(anywhere, anywhere),
         scratch_shapes=[
             pltpu.VMEM(primal.shape, f32),
             pltpu.VMEM(primal.shape, f32),
+            pltpu.VMEM(guess.shape, f32),
             pltpu.VMEM(primal.shape, f32),
-            pltpu.VMEM((2,) + plane, f32),
+            pltpu.VMEM(guess.shape, f32),
+            pltpu.VMEM(primal.shape, f32),
+            pltpu.VMEM((2,) + padded, f32),
             pltpu.VMEM((2, 2, fields, ny, nz), f32),
             pltpu.VMEM((2,) + plane, f32),
             pltpu.VMEM((2,) + plane, f32),
@@ -291,6 +324,9 @@
             pltpu.VMEM(plane, f32),
             dma((steps,)),
             dma((steps,)),
+            dma,
+            dma((steps,)),
+            dma,
             dma((2, 2, groups)),
             dma((2, 2, groups)),
             dma((2, nx)),
@@ -299,7 +335,7 @@
             dma((nx,)),
         ],
         compiler_params=pltpu.CompilerParams(
-            collective_id=0, has_side_effects=True, vmem_limit_bytes=40 * 2**20),
+            collective_id=0, has_side_effects=True, vmem_limit_bytes=60 * 2**20),
     )(primal, source, guess, mixing)
 
 

time: 109 us -> 105 us (0.963)
  the two profiles are of different devices: /device:TPU:26 before, /device:TPU:30 now
where the time goes in v1:
time: 105 us
  Pallas kernels  100 us (95%)
  local copies, waits for them, and re-layouts  4.31 us (4%)
    pallas_call x1, Pallas kernels, per_device(): pl.pallas_call(functools.partial(kernel, blocks, slabs), out_shape=(jax.S...  100 us
    unnamed x4, local copies, waits for them, and re-layouts  4.31 us

profile of v1, /device:TPU:30, one launch (start us, length us, event | category | flops | bytes accessed | tf_op | source)
XLA Modules:
  0.0 105.2 jit_solution(501352542705491387)
XLA Ops:
  0.6 100.3 %shard_map.59 = (f32[8,5,8,16,128]{4,3,2,1,0:T(8,128)}, f32[1,5,8,16,128]{4,3,2,1,0:T(8,128)}) custom-call(f32[8,5,8,16,128]{4,3,2,1,0:T(8,128)} %primal_hbm.1, f32[8,5,8,16,128]{4,3,2,1,0:T(8,128)} %source_hbm.1, f32[1,5,8,16,128]{4,3,2,1,0:T(8,128)} %guess_hbm.1, f32[5,5]{1,0:T(8,128)} %mixing.1), custom_call_target="tpu_custom_call" | custom-call | tf_op jit(solution)/shard_map/pallas_call | solution.py:306
  100.9 0.0 copy-start
  100.9 3.6 %copy.8 = f32[8,5,8,16,128]{4,3,2,1,0:T(8,128)} copy(f32[8,5,8,16,128]{4,3,2,1,0:T(8,128)} %get-tuple-element.4) | data formatting | bytes 5242880
  104.5 0.0 copy-done
  104.5 0.7 copy.9
Async XLA Ops:
  100.9 3.6 %copy-start = (f32[1,5,8,16,128]{4,3,2,1,0:T(8,128)S(1)}, f32[1,5,8,16,128]{4,3,2,1,0:T(8,128)}, u32[]{:S(2)}) copy-start(f32[1,5,8,16,128]{4,3,2,1,0:T(8,128)} %get-tuple-element.5) | copy-start | bytes 983044

commit v2 on v1

--- a/solution.py
+++ b/solution.py
@@ -16,9 +16,11 @@
 PAD = 8
 
 
-def kernel(blocks, slabs, primal_hbm, source_hbm, guess_hbm, mixing, fine_hbm, residual_hbm,
-           primal, source, guess, fine, residual_out, scaled, state, halo, ends, end_in, relaxed, moved, moved_in,
-           load_p, load_s, load_g, store_f, store_r, halo_send, halo_recv, end_send, end_recv, err_send, err_recv):
+def kernel(blocks, slabs, team, primal_hbm, source_hbm, guess_hbm, mixing, fine, residual_out,
+           primal, source, guess, scaled, state, halo, ends, end_in, relaxed, moved, moved_in,
+           slabs_in, far_in, far_out,
+           load_p, load_s, load_g, halo_send, halo_recv, end_send, end_recv, err_send, err_recv,
+           slab_send, slab_recv, far_send, far_recv, tree_send):
     steps, fields, nx, ny, nz = primal.shape
     last = nx - 1
     position = lax.axis_index("tm")
@@ -27,6 +29,17 @@
     edge = {LEFT: 0, RIGHT: last}
     first_block = position == 0
     has_next = position < blocks - 1
+    member = lax.rem(position, team)
+    closes_team = member == team - 1
+    first_team = position < team
+    last_team = position >= blocks - team
+    depth = team.bit_length() - 1
+
+    def is_parent(b):
+        return lax.rem(position, 2 << b) == (2 << b) - 1
+
+    def is_child(b):
+        return lax.rem(position, 2 << b) == (1 << b) - 1
     groups = halo_send.shape[-1]
     cuts = [(g * fields) // groups for g in range(groups + 1)]
 
@@ -36,11 +49,7 @@
     def load_source(t):
         return pltpu.make_async_copy(source_hbm.at[t], source.at[t], load_s.at[t])
 
-    def store_fine(t):
-        return pltpu.make_async_copy(fine.at[t], fine_hbm.at[t], store_f.at[t])
-
     load_guess = pltpu.make_async_copy(guess_hbm, guess, load_g)
-    store_residual = pltpu.make_async_copy(residual_out, residual_hbm, store_r)
     load_guess.start()
     load_primal(0).start()
     load_source(0).start()
@@ -52,15 +61,24 @@
     for way in (LEFT, RIGHT):
         pl.semaphore_signal(barrier, inc=1, device_id={"space": side[way]}, device_id_type=MESH)
 
-    @pl.when(has_next)
-    def _():
-        pl.semaphore_signal(barrier, inc=1, device_id={"tm": position + 1}, device_id_type=MESH)
-
-    @pl.when(jnp.logical_not(first_block))
-    def _():
-        pl.semaphore_signal(barrier, inc=1, device_id={"tm": position - 1}, device_id_type=MESH)
-
-    pl.semaphore_wait(barrier, 2 + jnp.where(first_block, 0, 1) + jnp.where(has_next, 1, 0))
+    peers = [
+        (jnp.logical_not(first_block), -1),
+        (has_next, 1),
+        (jnp.logical_and(closes_team, jnp.logical_not(first_team)), -team),
+        (jnp.logical_and(closes_team, jnp.logical_not(last_team)), team),
+    ]
+    for b in range(depth):
+        peers += [(is_parent(b), -(1 << b)), (is_child(b), 1 << b)]
+    expected = 2
+    for met, offset in peers:
+        expected = expected + jnp.where(met, 1, 0)
+
+        @pl.when(met)
+        def _():
+            pl.semaphore_signal(
+                barrier, inc=1, device_id={"tm": position + offset}, device_id_type=MESH)
+
+    pl.semaphore_wait(barrier, expected)
 
     weights = [[mixing[i, j] for j in range(fields)] for i in range(fields)]
 
@@ -106,6 +124,58 @@
             send_sem=err_send.at[x], recv_sem=err_recv.at[x],
             device_id={"tm": position + 1}, device_id_type=MESH,
         )
+
+    def slab_copy(src, j):
+        return pltpu.make_async_remote_copy(
+            src_ref=src, dst_ref=slabs_in.at[j],
+            send_sem=slab_send.at[j], recv_sem=slab_recv.at[j],
+            device_id={"tm": position + 1}, device_id_type=MESH,
+        )
+
+    def far_copy(x):
+        return pltpu.make_async_remote_copy(
+            src_ref=far_out.at[x], dst_ref=far_in.at[x],
+            send_sem=far_send.at[x], recv_sem=far_recv.at[x],
+            device_id={"tm": position + team}, device_id_type=MESH,
+        )
+
+    def tree_copy(b, x):
+        return pltpu.make_async_remote_copy(
+            src_ref=far_in.at[x], dst_ref=far_in.at[x],
+            send_sem=tree_send.at[b, x], recv_sem=far_recv.at[x],
+            device_id={"tm": position - (1 << b)}, device_id_type=MESH,
+        )
+
+    def send_slab():
+        @pl.when(jnp.logical_not(closes_team))
+        def _():
+            slab_copy(scaled.at[0], member).start()
+
+    def pass_slab(hop):
+        @pl.when(member >= hop)
+        def _():
+            j = member - hop
+            slab_copy(slabs_in.at[j], j).wait_recv()
+
+            @pl.when(jnp.logical_not(closes_team))
+            def _():
+                slab_copy(slabs_in.at[j], j).start()
+
+    def slopes(t):
+        load_primal(t).wait()
+
+        def slope(x, carry):
+            values = [primal[t, f, x] for f in range(fields)]
+            for f in range(fields):
+                bent = jnp.tanh(mix(values, f))
+                scaled[t, f, x] = RATE - RATE * (bent * bent)
+            return carry
+
+        lax.fori_loop(0, nx, slope, 0, unroll=2)
+
+    def coarse(slope, values):
+        return [(1.0 - COARSE_STEP) * values[f]
+                + (COARSE_STEP / RATE) * (slope[f] * mix(values, f)) for f in range(fields)]
 
     def stepped(slot, t, x, near):
         values = [state[slot, x, f, body] for f in range(fields)]
@@ -120,6 +190,8 @@
             results.append(KEEP * v + DIFFUSION * around + scaled[t, f, x] * mix(values, f))
         return results
 
+    early = (1, last - 1)
+
     def step(m, slot, t, ways, closing):
         final = m == 2
 
@@ -135,32 +207,21 @@
             if not closing:
                 state[1 - slot, x, f, body] = value
 
-        if m == 0:
-            load_primal(t).wait()
-            if not closing:
-                load_source(t + 1).wait()
-
-            def slope(x, carry):
-                values = [primal[t, f, x] for f in range(fields)]
-                for f in range(fields):
-                    bent = jnp.tanh(mix(values, f))
-                    scaled[t, f, x] = RATE - RATE * (bent * bent)
-                return carry
-
-            lax.fori_loop(0, nx, slope, 0, unroll=2)
-
-        def inner(x, carry):
+        if m == 0 and not closing:
+            load_source(t + 1).wait()
+            slopes(t + 1)
+
+        def inner(x):
             results = stepped(slot, t, x, (x - 1, x + 1))
             for f in range(fields):
                 put(x, f, given(x, f, results[f]))
-            if closing and not final:
+
+        for x in range(1, last):
+            inner(x)
+            if closing and not final and x in early:
                 @pl.when(has_next)
                 def _():
                     end_copy(m, x).start()
-            return carry
-
-        for x in range(1, last):
-            inner(x, 0)
         waiting = []
         for way in ways:
             target = RIGHT if way == LEFT else LEFT
@@ -178,15 +239,19 @@
                 @pl.when(has_next)
                 def _():
                     end_copy(m, x).start()
+        if closing and not final:
+            @pl.when(has_next)
+            def _():
+                for x in range(1, last):
+                    if x not in early:
+                        end_copy(m, x).start()
         for way in ways:
             for g in range(groups):
                 halo_copy(way, slot, g).wait_send()
-        if final:
-            store_fine(t + 1).start()
 
     forward, backward = (LEFT, RIGHT), (RIGHT, LEFT)
 
-    def march(m, count):
+    def march(m, count, between=()):
         pairs = (count - 1) // 2
 
         def pair(i, carry):
@@ -195,6 +260,8 @@
             return carry
 
         lax.fori_loop(0, pairs, pair, 0)
+        for hop in between:
+            pass_slab(hop)
         for t in range(2 * pairs, count):
             step(m, t % 2, t, (forward, backward)[t % 2], t == count - 1)
 
@@ -220,8 +287,10 @@
 
     load_guess.wait()
     begin(from_guess)
+    slopes(0)
+    send_slab()
     load_source(0).wait()
-    march(0, steps)
+    march(0, steps, (1,) if team > 2 else ())
 
     def from_end(x):
         @pl.when(first_block)
@@ -240,9 +309,14 @@
                 relaxed[x, f] = value
 
     begin(from_end)
-    march(1, steps)
-
-    def from_error(x):
+    march(1, steps, range(2, team - 1))
+
+    def last_slab():
+        @pl.when(closes_team)
+        def _():
+            slab_copy(slabs_in.at[0], 0).wait_recv()
+
+    def near(x):
         @pl.when(first_block)
         def _():
             for f in range(fields):
@@ -258,41 +332,108 @@
                 value = end_in[1, x, f] + source[0, f, x] - relaxed[x, f]
                 residual_out[0, f, x] = value
                 rest.append(value)
-            err_copy(x).wait_recv()
-            for f in range(fields):
-                moved_in[x, f] = moved_in[x, f] + rest[f]
+
+            @pl.when(member == 0)
+            def _():
+                for f in range(fields):
+                    moved_in[x, f] = rest[f]
+
+            @pl.when(member > 0)
+            def _():
+                err_copy(x).wait_recv()
+                for f in range(fields):
+                    moved_in[x, f] = moved_in[x, f] + rest[f]
+
+        @pl.when(jnp.logical_not(closes_team))
+        def _():
+            error = coarse([scaled[0, f, x] for f in range(fields)],
+                           [moved_in[x, f] for f in range(fields)])
+            for f in range(fields):
+                moved[x, f] = error[f]
+            err_copy(x).start()
+
+    def from_error(x):
+        @pl.when(closes_team)
+        def _():
+            near(x)
+
+        @pl.when(jnp.logical_not(first_team))
+        def _():
+            far_copy(x).wait_recv()
+
+            def through(j, values):
+                return tuple(coarse([slabs_in[j, f, x] for f in range(fields)], list(values)))
+
+            values = lax.fori_loop(
+                0, member, through, tuple(far_in[x, f] for f in range(fields)))
+            for f in range(fields):
+                moved_in[x, f] = moved_in[x, f] + values[f]
 
         error = [moved_in[x, f] for f in range(fields)]
 
-        @pl.when(has_next)
-        def _():
-            for f in range(fields):
-                moved[x, f] = (1.0 - COARSE_STEP) * error[f] + (COARSE_STEP / RATE) * (
-                    scaled[0, f, x] * mix(error, f))
-            err_copy(x).start()
+        @pl.when(jnp.logical_and(closes_team, jnp.logical_not(last_team)))
+        def _():
+            going = coarse([scaled[0, f, x] for f in range(fields)], error)
+            for f in range(fields):
+                far_out[x, f] = going[f]
+            far_copy(x).start()
+
+        for b in reversed(range(depth)):
+            @pl.when(jnp.logical_and(is_parent(b), jnp.logical_not(first_team)))
+            def _():
+                tree_copy(b, x).start()
 
         for f in range(fields):
             value = relaxed[x, f] + error[f]
             state[0, x, f, body] = value
             fine[0, f, x] = value
 
+    last_slab()
+
+    @pl.when(jnp.logical_not(closes_team))
+    def _():
+        near(0)
+        near(last)
+
+        def rest(x, carry):
+            near(x)
+            return carry
+
+        lax.fori_loop(1, last, rest, 0)
+
     begin(from_error)
-    store_fine(0).start()
-    store_residual.start()
     march(2, steps - 1)
-    for t in range(steps):
-        store_fine(t).wait()
-    store_residual.wait()
-
-    @pl.when(has_next)
-    def _():
-        def drain(x, carry):
+
+    def drain(x, carry):
+        @pl.when(has_next)
+        def _():
             end_copy(0, x).wait_send()
             end_copy(1, x).wait_send()
+
+        @pl.when(jnp.logical_not(closes_team))
+        def _():
             err_copy(x).wait_send()
+
+        @pl.when(jnp.logical_and(closes_team, jnp.logical_not(last_team)))
+        def _():
+            far_copy(x).wait_send()
+
+        for b in range(depth):
+            @pl.when(jnp.logical_and(is_parent(b), jnp.logical_not(first_team)))
+            def _():
+                tree_copy(b, x).wait_send()
+        return carry
+
+    lax.fori_loop(0, nx, drain, 0)
+
+    @pl.when(jnp.logical_not(closes_team))
+    def _():
+        def drain_slab(j, carry):
+            slab_copy(slabs_in.at[j], j).wait_send()
             return carry
 
-        lax.fori_loop(0, nx, drain, 0)
+        lax.fori_loop(0, member, drain_slab, 0)
+        slab_copy(scaled.at[0], member).wait_send()
 
 
 def per_device(blocks, slabs, primal, source, guess, mixing):
@@ -300,18 +441,20 @@
     groups = 2
     plane = (nx, fields, ny, nz)
     padded = (nx, fields, ny + 2 * PAD, nz)
-    anywhere = pl.BlockSpec(memory_space=pl.ANY)
+    hbm = pl.BlockSpec(memory_space=pltpu.HBM)
+    vmem = pl.BlockSpec(memory_space=pltpu.VMEM)
+    team = 2
+    while (2 * team) ** 2 <= blocks and blocks % (2 * team) == 0:
+        team *= 2
     dma = pltpu.SemaphoreType.DMA
     f32 = jnp.float32
     return pl.pallas_call(
-        functools.partial(kernel, blocks, slabs),
+        functools.partial(kernel, blocks, slabs, team),
         out_shape=(jax.ShapeDtypeStruct(primal.shape, f32), jax.ShapeDtypeStruct(guess.shape, f32)),
-        in_specs=[anywhere] * 3 + [pl.BlockSpec(memory_space=pltpu.SMEM)],
-        out_specs=(anywhere, anywhere),
+        in_specs=[hbm] * 3 + [pl.BlockSpec(memory_space=pltpu.SMEM)],
+        out_specs=(vmem, vmem),
         scratch_shapes=[
             pltpu.VMEM(primal.shape, f32),
-            pltpu.VMEM(primal.shape, f32),
-            pltpu.VMEM(guess.shape, f32),
             pltpu.VMEM(primal.shape, f32),
             pltpu.VMEM(guess.shape, f32),
             pltpu.VMEM(primal.shape, f32),
@@ -322,9 +465,10 @@
             pltpu.VMEM(plane, f32),
             pltpu.VMEM(plane, f32),
             pltpu.VMEM(plane, f32),
+            pltpu.VMEM((team - 1,) + primal.shape[1:], f32),
+            pltpu.VMEM(plane, f32),
+            pltpu.VMEM(plane, f32),
             dma((steps,)),
-            dma((steps,)),
-            dma,
             dma((steps,)),
             dma,
             dma((2, 2, groups)),
@@ -333,9 +477,14 @@
             dma((2, nx)),
             dma((nx,)),
             dma((nx,)),
+            dma((team,)),
+            dma((team,)),
+            dma((nx,)),
+            dma((nx,)),
+            dma((team.bit_length() - 1, nx)),
         ],
         compiler_params=pltpu.CompilerParams(
-            collective_id=0, has_side_effects=True, vmem_limit_bytes=60 * 2**20),
+            collective_id=0, has_side_effects=True, vmem_limit_bytes=48 * 2**20),
     )(primal, source, guess, mixing)
 
 

time: 105 us -> 95.2 us (0.907)
  the two profiles are of different devices: /device:TPU:30 before, /device:TPU:24 now
where the time goes in v2:
time: 95.2 us; the launch traced here: 95 us
  Pallas kernels  88.8 us (93%)
  local copies, waits for them, and re-layouts  5.61 us (6%)
    pallas_call x1, Pallas kernels, per_device(): pl.pallas_call(functools.partial(kernel, blocks, slabs, team), out_shape=...  88.8 us
    unnamed x8, local copies, waits for them, and re-layouts  5.61 us

profile of v2, /device:TPU:24, one launch (start us, length us, event | category | flops | bytes accessed | tf_op | source)
XLA Modules:
  0.0 95.0 jit_solution(3126714398683201418)
XLA Ops:
  0.6 0.0 copy-start
  0.6 1.7 %copy-done = f32[8,5,8,16,128]{4,3,2,1,0:T(8,128)S(1)} copy-done((f32[8,5,8,16,128]{4,3,2,1,0:T(8,128)S(1)}, f32[8,5,8,16,128]{4,3,2,1,0:T(8,128)}, u32[]{:S(2)}) %copy-start) | copy-done | bytes 2621464
  2.4 0.0 copy-start.1
  2.4 1.0 %copy-done.1 = f32[1,5,8,16,128]{4,3,2,1,0:T(8,128)S(1)} copy-done((f32[1,5,8,16,128]{4,3,2,1,0:T(8,128)S(1)}, f32[1,5,8,16,128]{4,3,2,1,0:T(8,128)}, u32[]{:S(2)}) %copy-start.1) | copy-done | bytes 327704
  3.3 0.0 copy-start.2
  3.3 0.7 copy-done.2
  4.0 88.8 %shard_map.59 = (f32[8,5,8,16,128]{4,3,2,1,0:T(8,128)S(1)}, f32[1,5,8,16,128]{4,3,2,1,0:T(8,128)S(1)}) custom-call(f32[8,5,8,16,128]{4,3,2,1,0:T(8,128)S(1)} %copy-done, f32[8,5,8,16,128]{4,3,2,1,0:T(8,128)} %source_hbm.1, f32[1,5,8,16,128]{4,3,2,1,0:T(8,128)S(1)} %copy-done.1, f32[5,5]{1,0:T(8,128)S(1)} %copy-done.2), custom_call_target="tpu_custom_call" | custom-call | tf_op jit(solution)/shard_map/pallas_call | solution.py:451
  92.8 1.5 %copy.8 = f32[8,5,8,16,128]{4,3,2,1,0:T(8,128)} copy(f32[8,5,8,16,128]{4,3,2,1,0:T(8,128)S(1)} %get-tuple-element.4) | data formatting | bytes 5242880
  94.3 0.7 copy.9
Async XLA Ops:
  0.6 1.7 %copy-start = (f32[8,5,8,16,128]{4,3,2,1,0:T(8,128)S(1)}, f32[8,5,8,16,128]{4,3,2,1,0:T(8,128)}, u32[]{:S(2)}) copy-start(f32[8,5,8,16,128]{4,3,2,1,0:T(8,128)} %primal_hbm.1) | copy-start | bytes 7864324
  2.4 1.0 %copy-start.1 = (f32[1,5,8,16,128]{4,3,2,1,0:T(8,128)S(1)}, f32[1,5,8,16,128]{4,3,2,1,0:T(8,128)}, u32[]{:S(2)}) copy-start(f32[1,5,8,16,128]{4,3,2,1,0:T(8,128)} %guess_hbm.1) | copy-start | bytes 983044
  3.3 0.7 copy-start.2

commit v3 on v2

--- a/solution.py
+++ b/solution.py
@@ -16,10 +16,10 @@
 PAD = 8
 
 
-def kernel(blocks, slabs, team, primal_hbm, source_hbm, guess_hbm, mixing, fine, residual_out,
-           primal, source, guess, scaled, state, halo, ends, end_in, relaxed, moved, moved_in,
+def kernel(blocks, slabs, team, primal_hbm, source_hbm, guess_hbm, mixing, fine_hbm, residual_hbm,
+           primal, source, guess, fine, residual_out, scaled, state, halo, ends, end_in, relaxed, moved, moved_in,
            slabs_in, far_in, far_out,
-           load_p, load_s, load_g, halo_send, halo_recv, end_send, end_recv, err_send, err_recv,
+           load_p, load_s, load_g, store_f, store_r, halo_send, halo_recv, end_send, end_recv, err_send, err_recv,
            slab_send, slab_recv, far_send, far_recv, tree_send):
     steps, fields, nx, ny, nz = primal.shape
     last = nx - 1
@@ -49,6 +49,10 @@
     def load_source(t):
         return pltpu.make_async_copy(source_hbm.at[t], source.at[t], load_s.at[t])
 
+    def store_fine(t):
+        return pltpu.make_async_copy(fine.at[t], fine_hbm.at[t], store_f.at[t])
+
+    store_residual = pltpu.make_async_copy(residual_out, residual_hbm, store_r)
     load_guess = pltpu.make_async_copy(guess_hbm, guess, load_g)
     load_guess.start()
     load_primal(0).start()
@@ -100,10 +104,11 @@
 
     lax.fori_loop(0, nx, clear, 0)
 
-    def halo_copy(way, slot, g):
+    def halo_copy(way, slot, g, given=False):
         part = pl.ds(cuts[g], cuts[g + 1] - cuts[g])
         return pltpu.make_async_remote_copy(
-            src_ref=state.at[slot, edge[way], part, body],
+            src_ref=guess_hbm.at[0, part, edge[way]] if given
+            else state.at[slot, edge[way], part, body],
             dst_ref=halo.at[way, slot, part],
             send_sem=halo_send.at[way, slot, g],
             recv_sem=halo_recv.at[way, slot, g],
@@ -248,6 +253,8 @@
         for way in ways:
             for g in range(groups):
                 halo_copy(way, slot, g).wait_send()
+        if final:
+            store_fine(t + 1).start()
 
     forward, backward = (LEFT, RIGHT), (RIGHT, LEFT)
 
@@ -285,8 +292,16 @@
         for f in range(fields):
             state[0, x, f, body] = guess[0, f, x]
 
+    for way in (LEFT, RIGHT):
+        for g in range(groups):
+            halo_copy(way, 0, g, True).start()
     load_guess.wait()
-    begin(from_guess)
+
+    def copy_guess(x, carry):
+        from_guess(x)
+        return carry
+
+    lax.fori_loop(0, nx, copy_guess, 0)
     slopes(0)
     send_slab()
     load_source(0).wait()
@@ -402,7 +417,13 @@
         lax.fori_loop(1, last, rest, 0)
 
     begin(from_error)
+    store_fine(0).start()
+    store_residual.start()
     march(2, steps - 1)
+
+    for t in range(steps):
+        store_fine(t).wait()
+    store_residual.wait()
 
     def drain(x, carry):
         @pl.when(has_next)
@@ -434,6 +455,16 @@
 
         lax.fori_loop(0, member, drain_slab, 0)
         slab_copy(scaled.at[0], member).wait_send()
+
+
+def hand_out(fine, residual, fine_out, residual_out, fine_sem, residual_sem):
+    copies = [pltpu.make_async_copy(fine.at[t], fine_out.at[t], fine_sem.at[t])
+              for t in range(fine.shape[0])]
+    copies.append(pltpu.make_async_copy(residual, residual_out, residual_sem))
+    for copy in copies:
+        copy.start()
+    for copy in copies:
+        copy.wait()
 
 
 def per_device(blocks, slabs, primal, source, guess, mixing):
@@ -442,19 +473,20 @@
     plane = (nx, fields, ny, nz)
     padded = (nx, fields, ny + 2 * PAD, nz)
     hbm = pl.BlockSpec(memory_space=pltpu.HBM)
-    vmem = pl.BlockSpec(memory_space=pltpu.VMEM)
     team = 2
     while (2 * team) ** 2 <= blocks and blocks % (2 * team) == 0:
         team *= 2
     dma = pltpu.SemaphoreType.DMA
     f32 = jnp.float32
-    return pl.pallas_call(
+    fine, residual = pl.pallas_call(
         functools.partial(kernel, blocks, slabs, team),
         out_shape=(jax.ShapeDtypeStruct(primal.shape, f32), jax.ShapeDtypeStruct(guess.shape, f32)),
         in_specs=[hbm] * 3 + [pl.BlockSpec(memory_space=pltpu.SMEM)],
-        out_specs=(vmem, vmem),
+        out_specs=(hbm, hbm),
         scratch_shapes=[
             pltpu.VMEM(primal.shape, f32),
+            pltpu.VMEM(primal.shape, f32),
+            pltpu.VMEM(guess.shape, f32),
             pltpu.VMEM(primal.shape, f32),
             pltpu.VMEM(guess.shape, f32),
             pltpu.VMEM(primal.shape, f32),
@@ -471,6 +503,8 @@
             dma((steps,)),
             dma((steps,)),
             dma,
+            dma((steps,)),
+            dma,
             dma((2, 2, groups)),
             dma((2, 2, groups)),
             dma((2, nx)),
@@ -484,8 +518,16 @@
             dma((team.bit_length() - 1, nx)),
         ],
         compiler_params=pltpu.CompilerParams(
-            collective_id=0, has_side_effects=True, vmem_limit_bytes=48 * 2**20),
+            collective_id=0, has_side_effects=True, vmem_limit_bytes=58 * 2**20),
     )(primal, source, guess, mixing)
+    return pl.pallas_call(
+        hand_out,
+        out_shape=(jax.ShapeDtypeStruct(primal.shape, f32), jax.ShapeDtypeStruct(guess.shape, f32)),
+        in_specs=[hbm] * 2,
+        out_specs=(hbm, hbm),
+        scratch_shapes=[dma((steps,)), dma],
+        compiler_params=pltpu.CompilerParams(vmem_limit_bytes=58 * 2**20),
+    )(fine, residual)
 
 
 def solution(mesh):

time: 95.2 us -> 180 us (1.89)
  Pallas kernels: 88.8 us -> 180 us
  local copies, waits for them, and re-layouts: 5.61 us -> 0 us
    pallas_call x0 -> x1, Pallas kernels: none -> 90.5 us  [per_device(): pl.pallas_call(hand_out, out_shape=(jax.ShapeDtypeStruct(primal.shape, f3...]
    unnamed x8 -> x0, local copies, waits for them, and re-layouts: 5.61 us -> none
where the time goes in v3:
time: 180 us
  Pallas kernels  180 us (100%)
    pallas_call x1, Pallas kernels, per_device(): pl.pallas_call(hand_out, out_shape=(jax.ShapeDtypeStruct(primal.shape, f3...  90.5 us
    pallas_call x1, Pallas kernels, per_device(): pl.pallas_call(functools.partial(kernel, blocks, slabs, team), out_shape=...  89 us

profile of v3, /device:TPU:24, one launch (start us, length us, event | category | flops | bytes accessed | tf_op | source)
XLA Modules:
  0.0 180.2 jit_solution(4895816447418262039)
XLA Ops:
  0.6 89.0 %shard_map.59 = (f32[8,5,8,16,128]{4,3,2,1,0:T(8,128)}, f32[1,5,8,16,128]{4,3,2,1,0:T(8,128)}) custom-call(f32[8,5,8,16,128]{4,3,2,1,0:T(8,128)} %primal_hbm.1, f32[8,5,8,16,128]{4,3,2,1,0:T(8,128)} %source_hbm.1, f32[1,5,8,16,128]{4,3,2,1,0:T(8,128)} %guess_hbm.1, f32[5,5]{1,0:T(8,128)} %mixing.1), custom_call_target="tpu_custom_call" | custom-call | tf_op jit(solution)/shard_map/pallas_call | solution.py:481
  89.6 90.5 %shard_map.60 = (f32[8,5,8,16,128]{4,3,2,1,0:T(8,128)}, f32[1,5,8,16,128]{4,3,2,1,0:T(8,128)}) custom-call(f32[8,5,8,16,128]{4,3,2,1,0:T(8,128)} %get-tuple-element.4.fine, f32[1,5,8,16,128]{4,3,2,1,0:T(8,128)} %get-tuple-element.5.residual), custom_call_target="tpu_custom_call" | custom-call | tf_op jit(solution)/shard_map/pallas_call | solution.py:523

commit v4 on v3

--- a/solution.py
+++ b/solution.py
@@ -123,10 +123,14 @@
             device_id={"tm": position + 1}, device_id_type=MESH,
         )
 
-    def err_copy(x):
+    def pieces(x):
+        cut = err_send.shape[-1] if isinstance(x, int) else 1
+        return [(h, pl.ds(h * (ny // cut), ny // cut)) for h in range(cut)]
+
+    def err_copy(x, h, part):
         return pltpu.make_async_remote_copy(
-            src_ref=moved.at[x], dst_ref=moved_in.at[x],
-            send_sem=err_send.at[x], recv_sem=err_recv.at[x],
+            src_ref=moved.at[x, :, part], dst_ref=moved_in.at[x, :, part],
+            send_sem=err_send.at[x, h], recv_sem=err_recv.at[x, h],
             device_id={"tm": position + 1}, device_id_type=MESH,
         )
 
@@ -137,17 +141,17 @@
             device_id={"tm": position + 1}, device_id_type=MESH,
         )
 
-    def far_copy(x):
+    def far_copy(x, h, part):
         return pltpu.make_async_remote_copy(
-            src_ref=far_out.at[x], dst_ref=far_in.at[x],
-            send_sem=far_send.at[x], recv_sem=far_recv.at[x],
+            src_ref=far_out.at[x, :, part], dst_ref=far_in.at[x, :, part],
+            send_sem=far_send.at[x, h], recv_sem=far_recv.at[x, h],
             device_id={"tm": position + team}, device_id_type=MESH,
         )
 
-    def tree_copy(b, x):
+    def tree_copy(b, x, h, part):
         return pltpu.make_async_remote_copy(
-            src_ref=far_in.at[x], dst_ref=far_in.at[x],
-            send_sem=tree_send.at[b, x], recv_sem=far_recv.at[x],
+            src_ref=far_in.at[x, :, part], dst_ref=far_in.at[x, :, part],
+            send_sem=tree_send.at[b, x, h], recv_sem=far_recv.at[x, h],
             device_id={"tm": position - (1 << b)}, device_id_type=MESH,
         )
 
@@ -331,87 +335,105 @@
         def _():
             slab_copy(slabs_in.at[0], 0).wait_recv()
 
-    def near(x):
+    def arrived(x):
+        @pl.when(jnp.logical_not(first_block))
+        def _():
+            end_copy(1, x).wait_recv()
+
+    def near(x, h, part):
         @pl.when(first_block)
         def _():
             for f in range(fields):
-                value = source[0, f, x]
-                residual_out[0, f, x] = value
-                moved_in[x, f] = value
+                value = source[0, f, x, part]
+                residual_out[0, f, x, part] = value
+                moved_in[x, f, part] = value
 
         @pl.when(jnp.logical_not(first_block))
         def _():
-            end_copy(1, x).wait_recv()
             rest = []
             for f in range(fields):
-                value = end_in[1, x, f] + source[0, f, x] - relaxed[x, f]
-                residual_out[0, f, x] = value
+                value = end_in[1, x, f, part] + source[0, f, x, part] - relaxed[x, f, part]
+                residual_out[0, f, x, part] = value
                 rest.append(value)
 
             @pl.when(member == 0)
             def _():
                 for f in range(fields):
-                    moved_in[x, f] = rest[f]
+                    moved_in[x, f, part] = rest[f]
 
             @pl.when(member > 0)
             def _():
-                err_copy(x).wait_recv()
+                err_copy(x, h, part).wait_recv()
                 for f in range(fields):
-                    moved_in[x, f] = moved_in[x, f] + rest[f]
+                    moved_in[x, f, part] = moved_in[x, f, part] + rest[f]
 
         @pl.when(jnp.logical_not(closes_team))
         def _():
-            error = coarse([scaled[0, f, x] for f in range(fields)],
-                           [moved_in[x, f] for f in range(fields)])
-            for f in range(fields):
-                moved[x, f] = error[f]
-            err_copy(x).start()
+            error = coarse([scaled[0, f, x, part] for f in range(fields)],
+                           [moved_in[x, f, part] for f in range(fields)])
+            for f in range(fields):
+                moved[x, f, part] = error[f]
+            err_copy(x, h, part).start()
+
+    def near_plane(x):
+        arrived(x)
+        for h, part in pieces(x):
+            near(x, h, part)
 
     def from_error(x):
         @pl.when(closes_team)
         def _():
-            near(x)
+            arrived(x)
+
+        for h, part in pieces(x):
+            corrected(x, h, part)
+
+    def corrected(x, h, part):
+        @pl.when(closes_team)
+        def _():
+            near(x, h, part)
 
         @pl.when(jnp.logical_not(first_team))
         def _():
-            far_copy(x).wait_recv()
+            far_copy(x, h, part).wait_recv()
 
             def through(j, values):
-                return tuple(coarse([slabs_in[j, f, x] for f in range(fields)], list(values)))
+                return tuple(
+                    coarse([slabs_in[j, f, x, part] for f in range(fields)], list(values)))
 
             values = lax.fori_loop(
-                0, member, through, tuple(far_in[x, f] for f in range(fields)))
-            for f in range(fields):
-                moved_in[x, f] = moved_in[x, f] + values[f]
-
-        error = [moved_in[x, f] for f in range(fields)]
+                0, member, through, tuple(far_in[x, f, part] for f in range(fields)))
+            for f in range(fields):
+                moved_in[x, f, part] = moved_in[x, f, part] + values[f]
+
+        error = [moved_in[x, f, part] for f in range(fields)]
 
         @pl.when(jnp.logical_and(closes_team, jnp.logical_not(last_team)))
         def _():
-            going = coarse([scaled[0, f, x] for f in range(fields)], error)
-            for f in range(fields):
-                far_out[x, f] = going[f]
-            far_copy(x).start()
+            going = coarse([scaled[0, f, x, part] for f in range(fields)], error)
+            for f in range(fields):
+                far_out[x, f, part] = going[f]
+            far_copy(x, h, part).start()
 
         for b in reversed(range(depth)):
             @pl.when(jnp.logical_and(is_parent(b), jnp.logical_not(first_team)))
             def _():
-                tree_copy(b, x).start()
+                tree_copy(b, x, h, part).start()
 
         for f in range(fields):
-            value = relaxed[x, f] + error[f]
-            state[0, x, f, body] = value
-            fine[0, f, x] = value
+            value = relaxed[x, f, part] + error[f]
+            state[0, x, f, pl.ds(PAD + part.start, part.size)] = value
+            fine[0, f, x, part] = value
 
     last_slab()
 
     @pl.when(jnp.logical_not(closes_team))
     def _():
-        near(0)
-        near(last)
+        near_plane(0)
+        near_plane(last)
 
         def rest(x, carry):
-            near(x)
+            near_plane(x)
             return carry
 
         lax.fori_loop(1, last, rest, 0)
@@ -431,21 +453,24 @@
             end_copy(0, x).wait_send()
             end_copy(1, x).wait_send()
 
-        @pl.when(jnp.logical_not(closes_team))
-        def _():
-            err_copy(x).wait_send()
-
-        @pl.when(jnp.logical_and(closes_team, jnp.logical_not(last_team)))
-        def _():
-            far_copy(x).wait_send()
-
-        for b in range(depth):
-            @pl.when(jnp.logical_and(is_parent(b), jnp.logical_not(first_team)))
-            def _():
-                tree_copy(b, x).wait_send()
+        for h, part in pieces(x):
+            @pl.when(jnp.logical_not(closes_team))
+            def _():
+                err_copy(x, h, part).wait_send()
+
+            @pl.when(jnp.logical_and(closes_team, jnp.logical_not(last_team)))
+            def _():
+                far_copy(x, h, part).wait_send()
+
+            for b in range(depth):
+                @pl.when(jnp.logical_and(is_parent(b), jnp.logical_not(first_team)))
+                def _():
+                    tree_copy(b, x, h, part).wait_send()
         return carry
 
-    lax.fori_loop(0, nx, drain, 0)
+    drain(0, 0)
+    drain(last, 0)
+    lax.fori_loop(1, last, drain, 0)
 
     @pl.when(jnp.logical_not(closes_team))
     def _():
@@ -457,19 +482,26 @@
         slab_copy(scaled.at[0], member).wait_send()
 
 
-def hand_out(fine, residual, fine_out, residual_out, fine_sem, residual_sem):
-    copies = [pltpu.make_async_copy(fine.at[t], fine_out.at[t], fine_sem.at[t])
+def hand_out(fine, residual, fine_out, residual_out, fine_held, residual_held,
+             fine_in, fine_sem, residual_in, residual_sem):
+    pieces = [(fine.at[t], fine_held.at[t], fine_out.at[t], fine_in.at[t], fine_sem.at[t])
               for t in range(fine.shape[0])]
-    copies.append(pltpu.make_async_copy(residual, residual_out, residual_sem))
-    for copy in copies:
-        copy.start()
-    for copy in copies:
-        copy.wait()
+    pieces.append((residual, residual_held, residual_out, residual_in, residual_sem))
+    loads = [pltpu.make_async_copy(src, held, sem) for src, held, _, sem, _ in pieces]
+    stores = [pltpu.make_async_copy(held, dst, sem) for _, held, dst, _, sem in pieces]
+    for load in loads:
+        load.start()
+    for load, store in zip(loads, stores):
+        load.wait()
+        store.start()
+    for store in stores:
+        store.wait()
 
 
 def per_device(blocks, slabs, primal, source, guess, mixing):
     steps, fields, nx, ny, nz = primal.shape
     groups = 2
+    halves = 2 if ny % 16 == 0 else 1
     plane = (nx, fields, ny, nz)
     padded = (nx, fields, ny + 2 * PAD, nz)
     hbm = pl.BlockSpec(memory_space=pltpu.HBM)
@@ -509,13 +541,13 @@
             dma((2, 2, groups)),
             dma((2, nx)),
             dma((2, nx)),
-            dma((nx,)),
-            dma((nx,)),
+            dma((nx, halves)),
+            dma((nx, halves)),
             dma((team,)),
             dma((team,)),
-            dma((nx,)),
-            dma((nx,)),
-            dma((team.bit_length() - 1, nx)),
+            dma((nx, halves)),
+            dma((nx, halves)),
+            dma((team.bit_length() - 1, nx, halves)),
         ],
         compiler_params=pltpu.CompilerParams(
             collective_id=0, has_side_effects=True, vmem_limit_bytes=58 * 2**20),
@@ -525,7 +557,14 @@
         out_shape=(jax.ShapeDtypeStruct(primal.shape, f32), jax.ShapeDtypeStruct(guess.shape, f32)),
         in_specs=[hbm] * 2,
         out_specs=(hbm, hbm),
-        scratch_shapes=[dma((steps,)), dma],
+        scratch_shapes=[
+            pltpu.VMEM(primal.shape, f32),
+            pltpu.VMEM(guess.shape, f32),
+            dma((steps,)),
+            dma((steps,)),
+            dma,
+            dma,
+        ],
         compiler_params=pltpu.CompilerParams(vmem_limit_bytes=58 * 2**20),
     )(fine, residual)
 

time: 180 us -> 92.9 us (0.52)
  Pallas kernels: 180 us -> 92.1 us
    pallas_call x1, Pallas kernels: 90.5 us -> 2.72 us  [per_device(): pl.pallas_call(hand_out, out_shape=(jax.ShapeDtypeStruct(primal.shape, f3...]
where the time goes in v4:
time: 92.9 us; the launch traced here: 92.7 us
  Pallas kernels  92.1 us (99%)
    pallas_call x1, Pallas kernels, per_device(): pl.pallas_call(functools.partial(kernel, blocks, slabs, team), out_shape=...  89.4 us
    pallas_call x1, Pallas kernels, per_device(): pl.pallas_call(hand_out, out_shape=(jax.ShapeDtypeStruct(primal.shape, f3...  2.72 us

profile of v4, /device:TPU:24, one launch (start us, length us, event | category | flops | bytes accessed | tf_op | source)
XLA Modules:
  0.0 92.7 jit_solution(4490466601988359062)
XLA Ops:
  0.6 89.4 %shard_map.59 = (f32[8,5,8,16,128]{4,3,2,1,0:T(8,128)}, f32[1,5,8,16,128]{4,3,2,1,0:T(8,128)}) custom-call(f32[8,5,8,16,128]{4,3,2,1,0:T(8,128)} %primal_hbm.1, f32[8,5,8,16,128]{4,3,2,1,0:T(8,128)} %source_hbm.1, f32[1,5,8,16,128]{4,3,2,1,0:T(8,128)} %guess_hbm.1, f32[5,5]{1,0:T(8,128)} %mixing.1), custom_call_target="tpu_custom_call" | custom-call | tf_op jit(solution)/shard_map/pallas_call | solution.py:513
  90.0 2.7 %shard_map.60 = (f32[8,5,8,16,128]{4,3,2,1,0:T(8,128)}, f32[1,5,8,16,128]{4,3,2,1,0:T(8,128)}) custom-call(f32[8,5,8,16,128]{4,3,2,1,0:T(8,128)} %get-tuple-element.4.fine, f32[1,5,8,16,128]{4,3,2,1,0:T(8,128)} %get-tuple-element.5.residual), custom_call_target="tpu_custom_call" | custom-call | tf_op jit(solution)/shard_map/pallas_call | solution.py:555

commit v5 on v4

--- a/solution.py
+++ b/solution.py
@@ -500,8 +500,8 @@
 
 def per_device(blocks, slabs, primal, source, guess, mixing):
     steps, fields, nx, ny, nz = primal.shape
-    groups = 2
-    halves = 2 if ny % 16 == 0 else 1
+    groups = fields
+    halves = 1
     plane = (nx, fields, ny, nz)
     padded = (nx, fields, ny + 2 * PAD, nz)
     hbm = pl.BlockSpec(memory_space=pltpu.HBM)

time: 92.9 us -> 89.1 us (0.959)
  Pallas kernels: 92.1 us -> 88.3 us
    pallas_call x1, Pallas kernels: 89.4 us -> 85.6 us  [per_device(): pl.pallas_call(functools.partial(kernel, blocks, slabs, team), out_shape=...]
where the time goes in v5:
time: 89.1 us; the launch traced here: 88.9 us
  Pallas kernels  88.3 us (99%)
    pallas_call x1, Pallas kernels, per_device(): pl.pallas_call(functools.partial(kernel, blocks, slabs, team), out_shape=...  85.6 us
    pallas_call x1, Pallas kernels, per_device(): pl.pallas_call(hand_out, out_shape=(jax.ShapeDtypeStruct(primal.shape, f3...  2.72 us

profile of v5, /device:TPU:24, one launch (start us, length us, event | category | flops | bytes accessed | tf_op | source)
XLA Modules:
  0.0 88.9 jit_solution(6603118072659417036)
XLA Ops:
  0.6 85.6 %shard_map.59 = (f32[8,5,8,16,128]{4,3,2,1,0:T(8,128)}, f32[1,5,8,16,128]{4,3,2,1,0:T(8,128)}) custom-call(f32[8,5,8,16,128]{4,3,2,1,0:T(8,128)} %primal_hbm.1, f32[8,5,8,16,128]{4,3,2,1,0:T(8,128)} %source_hbm.1, f32[1,5,8,16,128]{4,3,2,1,0:T(8,128)} %guess_hbm.1, f32[5,5]{1,0:T(8,128)} %mixing.1), custom_call_target="tpu_custom_call" | custom-call | tf_op jit(solution)/shard_map/pallas_call | solution.py:513
  86.2 2.7 %shard_map.60 = (f32[8,5,8,16,128]{4,3,2,1,0:T(8,128)}, f32[1,5,8,16,128]{4,3,2,1,0:T(8,128)}) custom-call(f32[8,5,8,16,128]{4,3,2,1,0:T(8,128)} %get-tuple-element.4.fine, f32[1,5,8,16,128]{4,3,2,1,0:T(8,128)} %get-tuple-element.5.residual), custom_call_target="tpu_custom_call" | custom-call | tf_op jit(solution)/shard_map/pallas_call | solution.py:555
